TPU v7x, 32 devices: a whole 2x2x4 slice. The times are simulated.
32 devices in a mesh: tm: 8 (over y, x, core), tile: 4 (over z).
Axes of the slice: x: 2, y: 2, z: 4, core: 2. Of those that a mesh axis runs over, the one named last changes fastest.
Arguments:
- velocity_u: float32 [384, 2, 16, 1024], P('tm', None, None, 'tile'), may hold values from -12 to 12
- velocity_v: float32 [384, 2, 16, 1024], P('tm', None, None, 'tile'), may hold values from -12 to 12
- land_sea: int32 [16, 1024], P(None, 'tile'), may hold values 0 or 1
- bottom_level: int32 [16, 1024], P(None, 'tile'), may hold values from 0 to 2
- spacing_x: float32 [16, 1024], P(None, 'tile'), may hold values from 0.5 to 2
- spacing_y: float32 [16, 1024], P(None, 'tile'), may hold values from 0.5 to 2
Outputs:
- conversion_maps: bfloat16 [384, 2, 16, 1024], P('tm', None, None, 'tile')
- mean_map: float32 [2, 16, 1024], P(None, None, 'tile')
All inputs are finite; a program needn't handle non-finite values. No bound on the sum of `land_sea` on one device may be relied on, other than what follows from the above.
Results may differ from a plain program's by a relative error of at most 0.001.
Values sent between devices are 32-bit elements; how exact they have to be, the bound alone decides.
A program may use at most 64 MiB of HBM per device.

v0:
```python
import jax
import jax.numpy as jnp
from jax import lax
from jax.sharding import PartitionSpec as P

HALF = 24
SNAPS = 48
cutoff_freq = 1.0 / 40.0


def extended(x, sides, width):
    for axis, dim in sides:
        size, length = (lax.axis_size(axis), x.shape[dim])
        up = [(i, (i + 1) % size) for i in range(size - 1)]
        down = [(j, i) for i, j in up]
        last = lax.slice_in_dim(x, length - width, length, axis=dim)
        first = lax.slice_in_dim(x, 0, width, axis=dim)
        before = lax.ppermute(last, axis, up)
        after = lax.ppermute(first, axis, down)
        x = jnp.concatenate([before, x, after], axis=dim)
    return x


def band_matrix(count):
    out_rows = jnp.arange(count, dtype=jnp.int32)[:, None]
    in_cols = jnp.arange(count + 2 * HALF, dtype=jnp.int32)[None, :]
    offset = (in_cols - out_rows - HALF).astype(jnp.float32)
    weights = 2.0 * cutoff_freq * jnp.sinc(2.0 * cutoff_freq * offset) * jnp.sinc(offset / HALF)
    return jnp.where(jnp.abs(offset) <= HALF, weights, jnp.zeros_like(weights))


def lowpass(padded, validity, blocks, block):
    matrix = band_matrix(block)

    def one_block(block_id):
        start = block_id * block
        window = lax.dynamic_slice_in_dim(padded, start, block + 2 * HALF, 0)
        valid_part = lax.dynamic_slice_in_dim(validity, start, block + 2 * HALF, 0)
        weighted = jnp.dot(
            matrix, window, precision=lax.Precision.HIGHEST, preferred_element_type=jnp.float32
        )
        weight_sum = jnp.dot(
            matrix, valid_part, precision=lax.Precision.HIGHEST, preferred_element_type=jnp.float32
        )
        return weighted / weight_sum[:, None]

    result = lax.map(one_block, jnp.arange(blocks, dtype=jnp.int32))
    return result.reshape(blocks * block, padded.shape[1])


def wet_cells(land_sea, bottom_level, levels):
    level_ids = jnp.arange(levels, dtype=jnp.int32)[:, None, None]
    return ((land_sea[None] == 1) & (level_ids < bottom_level[None])).astype(jnp.float32)


def filter_series(series):
    length = series.shape[0]
    flattened = series.reshape(length, -1)
    padded = jnp.pad(flattened, ((HALF, HALF), (0, 0)))
    validity = jnp.pad(jnp.ones((length,), jnp.float32), (HALF, HALF))
    return lowpass(padded, validity, length // SNAPS, SNAPS).reshape(series.shape)


def shards(velocity_u, velocity_v, land_sea, bottom_level, spacing_x, spacing_y):
    block_len = velocity_u.shape[0]
    total_len = block_len * lax.axis_size("tm")
    stacked = jnp.stack([velocity_u, velocity_v], axis=1)
    full_shape = stacked.shape
    flat_cells = stacked.reshape(block_len, 2, -1)
    series_mean = filter_series(
        lax.all_to_all(flat_cells, "tm", split_axis=2, concat_axis=0, tiled=True)
    )
    mean_flat = lax.all_to_all(series_mean, "tm", split_axis=0, concat_axis=2, tiled=True)
    mean_flow = mean_flat.reshape(full_shape)
    eddies = stacked - mean_flow
    wet_mask = wet_cells(land_sea, bottom_level, full_shape[2])
    masked = mean_flow * wet_mask[None, None]
    edge_cols = jnp.concatenate([masked[..., :1], masked[..., -1:]], axis=4)
    edge_ext = extended(edge_cols, (("tile", 4),), 1)
    left_col = edge_ext[..., :1]
    right_col = edge_ext[..., 3:4]
    ahead = jnp.concatenate([masked[..., 1:], right_col], axis=4)
    behind = jnp.concatenate([left_col, masked[..., :-1]], axis=4)
    grad_x = (ahead - behind) * (0.5 / spacing_x)
    row_padded = jnp.pad(masked, ((0, 0), (0, 0), (0, 0), (1, 1), (0, 0)))
    grad_y = (row_padded[..., 2:, :] - row_padded[..., :-2, :]) * (0.5 / spacing_y)
    eddy_u = eddies[:, 0]
    eddy_v = eddies[:, 1]
    total = (
        eddy_u * eddy_u * grad_x[:, 0]
        + eddy_u * eddy_v * (grad_y[:, 0] + grad_x[:, 1])
        + eddy_v * eddy_v * grad_y[:, 1]
    )
    conversion = -wet_mask[None] * total
    summed = lax.psum(jnp.sum(conversion, axis=0), "tm")
    return (conversion.astype(jnp.bfloat16), summed / total_len)


def solution(mesh):
    in_specs = (
        P("tm", None, None, "tile"),
        P("tm", None, None, "tile"),
        P(None, "tile"),
        P(None, "tile"),
        P(None, "tile"),
        P(None, "tile"),
    )
    out_specs = (P("tm", None, None, "tile"), P(None, None, "tile"))
    return jax.shard_map(shards, mesh=mesh, in_specs=in_specs, out_specs=out_specs, check_vma=False)
```

profile of v0, /device:TPU:0, one launch (start us, length us, event | category | flops | bytes accessed | tf_op | source)
XLA Modules:
  0.0 262.7 jit_solution(6098952019784487532)
XLA Ops:
  0.6 2.7 %stack.18 = f32[48,1,8192]{2,0,1:T(8,128)} reshape(f32[48,2,16,256]{3,2,1,0:T(8,128)} %param.9) | data formatting | bytes 3145728 | tf_op jit(solution)/shard_map/stack | solution.py:67
  6.9 8.0 %copy.21 = f32[48,2,8192]{0,1,2:T(2,128)} copy(f32[48,2,8192]{2,0,1:T(8,128)S(1)} %pad_maximum_fusion) | data formatting | bytes 6291456 | tf_op jit(solution)/shard_map/stack | solution.py:67
  14.9 16.2 %reshape.50 = f32[8,1,98304]{2,1,0:T(1,128)} reshape(f32[8192,2,48]{2,1,0:T(2,128)} %bitcast.49) | data formatting | bytes 6291456
  31.0 5.4 %all-to-all-start = ((f32[8,1,98304]{2,1,0:T(1,128)}), f32[8,1,98304]{2,1,0:T(1,128)S(1)}, u32[]{:S(2)}, u32[]{:S(2)}) async-start(f32[8,1,98304]{2,1,0:T(1,128)} %reshape.50), calls=%async_computation | async-start | bytes 6291456 | tf_op jit(solution)/shard_map/all_to_all | solution.py:71
  37.2 36.8 %all-to-all-done = f32[8,1,98304]{2,1,0:T(1,128)S(1)} async-done(((f32[8,1,98304]{2,1,0:T(1,128)}), f32[8,1,98304]{2,1,0:T(1,128)S(1)}, u32[]{:S(2)}, u32[]{:S(2)}) %all-to-all-start) | async-done | bytes 3145760 | tf_op jit(solution)/shard_map/all_to_all | solution.py:71
  74.6 11.2 %reduce = f32[8,98304]{1,0:T(8,128)} reduce(f32[8,1,98304]{2,1,0:T(1,128)S(1)} %all-to-all-done, f32[]{:T(128)} %broadcast.65), dimensions={1}, to_apply=%all_to_all.22.reduce_sub_computation | reduce | bytes 6291460 | tf_op jit(solution)/shard_map/all_to_all | solution.py:71
  85.8 19.3 %reshape.51 = f32[8192,2,48]{2,1,0:T(2,128)} reshape(f32[8,98304]{1,0:T(8,128)} %reduce) | data formatting | bytes 6291456
  105.1 7.0 %copy.30 = f32[48,2,8,1024]{3,2,0,1:T(8,128)S(1)} copy(f32[48,2,8,1024]{0,1,3,2:T(2,128)} %bitcast.50) | data formatting | bytes 6291456 | tf_op jit(solution)/shard_map/all_to_all | solution.py:71
  112.1 2.4 copy.23
  116.3 34.3 %while.11 = (s32[]{:T(128)}, f32[8,48,2048]{2,1,0:T(8,128)}, s32[8]{0:T(128)S(1)}, f32[432,2048]{1,0:T(8,128)S(1)}, f32[48,96]{1,0:T(8,128)}, /*index=5*/f32[432...) while((s32[]{:T(128)}, f32[8,48,2048]{2,1,0:T(8,128)}, s32[8]{0:T(128)S(1)}, ...), condition=%wide.region_1.3_spmd.clone, body=%wide.region_0.2_spmd.clone.sunk | while | flops 113399816 | bytes 1224551 | solution.py:47
  150.6 5.6 %reshape_reshape.3 = f32[384,2,1024]{2,1,0:T(2,128)} reshape(f32[8,48,2048]{2,1,0:T(8,128)} %get-tuple-element.38) | data formatting | bytes 6291456 | tf_op jit(solution)/shard_map/reshape;reshape | solution.py:61
  156.2 4.0 %all-to-all-start.1 = ((f32[384,2,1024]{2,1,0:T(2,128)}), f32[384,2,1024]{2,1,0:T(2,128)S(1)}, u32[]{:S(2)}, u32[]{:S(2)}) async-start(f32[384,2,1024]{2,1,0:T(2,128)} %reshape_reshape.3), calls=%async_computation.1 | async-start | bytes 6291456 | tf_op jit(solution)/shard_map/all_to_all | solution.py:73
  160.3 37.7 %all-to-all-done.1 = f32[384,2,1024]{2,1,0:T(2,128)S(1)} async-done(((f32[384,2,1024]{2,1,0:T(2,128)}), f32[384,2,1024]{2,1,0:T(2,128)S(1)}, u32[]{:S(2)}, u32[]{:S(2)}) %all-to-all-start.1) | async-done | bytes 3145760 | tf_op jit(solution)/shard_map/all_to_all | solution.py:73
  200.8 2.6 reshape.47
  203.4 5.7 %maximum_subtract_fusion = (f32[48,2,2,16,256]{4,3,2,1,0:T(8,128)}, f32[48,2,2,16,256]{4,3,2,1,0:T(8,128)S(1)}) fusion(f32[48,2,2,16,256]{4,3,2,1,0:T(8,128)} %reshape.47, f32[48,1,2,16,256]{4,3,2,1,0:T(8,128)} %bitcast.55, f32[48,1,2,16,256]{4,3,2,1,0:T(8,128)} %bitcast.56, f32[2,16,256]{2,1,0:T(8,128)S(1)} %fusion.15), kind=kLoop, calls=%fused_computation.12 | loop fusion | flops 2359296 | bytes 12615680 | tf_op jit(solution)/shard_map/sub | solution.py:75
  209.1 3.7 %fusion.47 = (f32[48,2,2,16,255]{4,3,2,1,0:T(8,128)}, f32[48,2,2,16,255]{4,3,2,1,0:T(8,128)}) fusion(f32[48,2,2,16,256]{4,3,2,1,0:T(8,128)S(1)} %get-tuple-element.70), kind=kLoop, calls=%fused_computation.85 | loop fusion | bytes 12533760 | tf_op jit(solution)/shard_map/slice | solution.py:83
  212.8 2.3 fusion.46
  218.6 2.2 copy.28
  220.8 4.7 %collective-permute-start.1 = (f32[48,2,2,16,1]{0,3,4,2,1:T(8,128)S(1)}, f32[48,2,2,16,1]{0,3,4,2,1:T(8,128)S(1)}, u32[]{:S(2)}, u32[]{:S(2)}) collective-permute-start(f32[48,2,2,16,1]{0,3,4,2,1:T(8,128)S(1)} %copy.28), channel_id=1, source_target_pairs={{0,1},{1,2},{2,3},{4,5},{5,6},{6,7},{8,9},{9,10},{10,11},{12,13},{... | collective-permute-start | bytes 36872 | tf_op jit(solution)/shard_map/ppermute | solution.py:18
  225.5 2.4 fusion.7
  228.0 2.4 copy.27
  230.3 2.4 copy.29
  232.7 4.3 %fusion.8 = f32[48,2,2,16,256]{4,3,2,1,0:T(8,128)S(1)} fusion(f32[48,2,2,16,1]{4,3,2,1,0:T(8,128)} %copy.27, f32[48,2,2,16,255]{4,3,2,1,0:T(8,128)} %get-tuple-element.74, f32[48,2,2,16,255]{4,3,2,1,0:T(8,128)S(1)} %copy-done.2, f32[48,2,2,16,1]{4,3,2,1,0:T(8,128)} %copy.29, f32[16,256]{1,0:T(8,128)S(1)} %broadcast_divide_fusion.1), kind=kLoop, calls=%fused_computation.15 | loop fusion | flops 3145728 | bytes 9453568 | tf_op jit(solution)/shard_map/mul | solution.py:84
  239.5 22.3 %psum.7 = f32[2,16,256]{2,1,0:T(8,128)S(1)} all-reduce(f32[2,16,256]{2,1,0:T(8,128)S(1)} %get-tuple-element.67), channel_id=1, replica_groups=mesh['tm'=8,'tile'=4] {'tm'}, use_global_device_ids=true, to_apply=%region_3.5 | all-reduce | flops 8192 | bytes 65536 | tf_op jit(solution)/shard_map/psum | solution.py:95
  (63 shorter events, 45.2 us)
Async XLA Ops:
  0.6 2.7 %copy-start.3 = (f32[48,2,16,256]{3,2,1,0:T(8,128)S(1)}, f32[48,2,16,256]{3,2,1,0:T(8,128)}, u32[]{:S(2)}) copy-start(f32[48,2,16,256]{3,2,1,0:T(8,128)} %param.10) | copy-start | bytes 4718596
  31.0 43.1 %all-to-all-start = ((f32[8,1,98304]{2,1,0:T(1,128)}), f32[8,1,98304]{2,1,0:T(1,128)S(1)}, u32[]{:S(2)}, u32[]{:S(2)}) async-start(f32[8,1,98304]{2,1,0:T(1,128)} %reshape.50), calls=%async_computation | async-start | bytes 6291456 | tf_op jit(solution)/shard_map/all_to_all | solution.py:71
  156.2 4.0 %copy-start.5 = (s32[16,256]{1,0:T(8,128)S(1)}, s32[16,256]{1,0:T(8,128)}, u32[]{:S(2)}) copy-start(s32[16,256]{1,0:T(8,128)} %param.11) | copy-start | bytes 49156
  156.2 4.0 %copy-start.6 = (f32[16,256]{1,0:T(8,128)S(1)}, f32[16,256]{1,0:T(8,128)}, u32[]{:S(2)}) copy-start(f32[16,256]{1,0:T(8,128)} %param.13) | copy-start | bytes 49156
  156.2 4.0 %copy-start.7 = (f32[16,256]{1,0:T(8,128)S(1)}, f32[16,256]{1,0:T(8,128)}, u32[]{:S(2)}) copy-start(f32[16,256]{1,0:T(8,128)} %param.14) | copy-start | bytes 49156
  156.2 4.1 %copy-start.4 = (s32[16,256]{1,0:T(8,128)S(1)}, s32[16,256]{1,0:T(8,128)}, u32[]{:S(2)}) copy-start(s32[16,256]{1,0:T(8,128)} %param.12) | copy-start | bytes 49156
  156.2 41.8 %all-to-all-start.1 = ((f32[384,2,1024]{2,1,0:T(2,128)}), f32[384,2,1024]{2,1,0:T(2,128)S(1)}, u32[]{:S(2)}, u32[]{:S(2)}) async-start(f32[384,2,1024]{2,1,0:T(2,128)} %reshape_reshape.3), calls=%async_computation.1 | async-start | bytes 6291456 | tf_op jit(solution)/shard_map/all_to_all | solution.py:73
  217.3 10.7 %collective-permute-start = (f32[48,2,2,16,1]{0,3,4,2,1:T(8,128)S(1)}, f32[48,2,2,16,1]{0,3,4,2,1:T(8,128)S(1)}, u32[]{:S(2)}, u32[]{:S(2)}) collective-permute-start(f32[48,2,2,16,1]{0,3,4,2,1:T(8,128)S(1)} %copy.26), channel_id=1, source_target_pairs={{1,0},{2,1},{3,2},{5,4},{6,5},{7,6},{9,8},{10,9},{11,10},{13,12},{... | collective-permute-start | bytes 36872 | tf_op jit(solution)/shard_map/ppermute | solution.py:19
  220.8 9.6 %collective-permute-start.1 = (f32[48,2,2,16,1]{0,3,4,2,1:T(8,128)S(1)}, f32[48,2,2,16,1]{0,3,4,2,1:T(8,128)S(1)}, u32[]{:S(2)}, u32[]{:S(2)}) collective-permute-start(f32[48,2,2,16,1]{0,3,4,2,1:T(8,128)S(1)} %copy.28), channel_id=1, source_target_pairs={{0,1},{1,2},{2,3},{4,5},{5,6},{6,7},{8,9},{9,10},{10,11},{12,13},{... | collective-permute-start | bytes 36872 | tf_op jit(solution)/shard_map/ppermute | solution.py:18
  228.0 4.7 %copy-start.2 = (f32[48,2,2,16,255]{4,3,2,1,0:T(8,128)S(1)}, f32[48,2,2,16,255]{4,3,2,1,0:T(8,128)}, u32[]{:S(2)}) copy-start(f32[48,2,2,16,255]{4,3,2,1,0:T(8,128)} %get-tuple-element.73) | copy-start | bytes 9400324
  232.7 4.3 %copy-start = (f32[48,2,2,16,256]{4,3,2,1,0:T(8,128)S(1)}, f32[48,2,2,16,256]{4,3,2,1,0:T(8,128)}, u32[]{:S(2)}) copy-start(f32[48,2,2,16,256]{4,3,2,1,0:T(8,128)} %fusion.7) | copy-start | bytes 9437188
  232.7 4.7 %copy-start.1 = (f32[48,2,2,16,256]{4,3,2,1,0:T(8,128)S(1)}, f32[48,2,2,16,256]{4,3,2,1,0:T(8,128)}, u32[]{:S(2)}) copy-start(f32[48,2,2,16,256]{4,3,2,1,0:T(8,128)} %get-tuple-element.69) | copy-start | bytes 9437188
where the time goes:
time: 267 us; the launch traced here: 263 us
  local copies, waits for them, and re-layouts  90.8 us (34%)
  waiting for transfers between devices  74.5 us (28%)
  other arithmetic  29.2 us (11%)
  matrix products  24.2 us (9%)
  blocking collectives  22.3 us (8%)
  starting transfers between devices  15.4 us (6%)
  loops' own time  5.18 us (2%)
    all_to_all x1, waiting for transfers between devices, shards(): lax.all_to_all(series_mean, 'tm', split_axis=0, concat_axis=2, tiled=True)  37.7 us
    unnamed x19, local copies, waits for them, and re-layouts  37.3 us
    all_to_all x1, waiting for transfers between devices, shards(): lax.all_to_all(flat_cells, 'tm', split_axis=2, concat_axis=0, tiled=True)  36.8 us
    psum x1, blocking collectives, shards(): summed = lax.psum(jnp.sum(conversion, axis=0), 'tm')  22.3 us
    dot_general x8, matrix products, one_block(): jnp.dot(matrix, window, precision=lax.Precision.HIGHEST, preferred_elemen...  16.8 us
    another operation x3, local copies, waits for them, and re-layouts, shards(): stacked = jnp.stack([velocity_u, velocity_v], axis=1)  12.1 us
    all_to_all x1, other arithmetic, shards(): lax.all_to_all(flat_cells, 'tm', split_axis=2, concat_axis=0, tiled=True)  11.2 us
    all_to_all x3, local copies, waits for them, and re-layouts, shards(): lax.all_to_all(flat_cells, 'tm', split_axis=2, concat_axis=0, tiled=True)  9.91 us
  transfers between devices with their start and end apart: 4, of which 2 were waited for; matrix products, arithmetic and copies ran while one was open for 3% of the time, Pallas kernels for 0%

commit v1 on v0

--- a/solution.py
+++ b/solution.py
@@ -70,7 +70,10 @@
     series_mean = filter_series(
         lax.all_to_all(flat_cells, "tm", split_axis=2, concat_axis=0, tiled=True)
     )
-    mean_flat = lax.all_to_all(series_mean, "tm", split_axis=0, concat_axis=2, tiled=True)
+    mean_flat = jnp.concatenate(
+        lax.all_to_all(jnp.stack(jnp.split(series_mean, lax.axis_size("tm"), axis=0)), "tm", 0, 0),
+        axis=2,
+    )
     mean_flow = mean_flat.reshape(full_shape)
     eddies = stacked - mean_flow
     wet_mask = wet_cells(land_sea, bottom_level, full_shape[2])

time: 267 us -> 289 us (1.082)
  local copies, waits for them, and re-layouts: 90.8 us -> 113 us
    another operation x1 -> x11, local copies, waits for them, and re-layouts: 5.6 us -> 21.3 us  [the longest x10 16.4 us: shards(): jnp.stack(jnp.split(series_mean, lax.axis_size('tm'), axis=0))]
    unnamed x19 -> x30, local copies, waits for them, and re-layouts: 37.3 us -> 42.4 us
    split x0 -> x1, local copies, waits for them, and re-layouts: none -> 3.24 us  [shards(): jnp.split(series_mean, lax.axis_size('tm'), axis=0)]
where the time goes in v1:
time: 289 us; the launch traced here: 284 us
  local copies, waits for them, and re-layouts  113 us (39%)
  waiting for transfers between devices  74.3 us (26%)
  other arithmetic  29.1 us (10%)
  matrix products  24.2 us (8%)
  blocking collectives  22.3 us (8%)
  starting transfers between devices  15.5 us (5%)
  loops' own time  4.79 us (2%)
    unnamed x30, local copies, waits for them, and re-layouts  42.4 us
    all_to_all x1, waiting for transfers between devices, shards(): lax.all_to_all(jnp.stack(jnp.split(series_mean, lax.axis_size('tm'), axis...  37.7 us
    all_to_all x1, waiting for transfers between devices, shards(): lax.all_to_all(flat_cells, 'tm', split_axis=2, concat_axis=0, tiled=True)  36.6 us
    psum x1, blocking collectives, shards(): summed = lax.psum(jnp.sum(conversion, axis=0), 'tm')  22.3 us
    dot_general x8, matrix products, one_block(): jnp.dot(matrix, window, precision=lax.Precision.HIGHEST, preferred_elemen...  16.7 us
    another operation x10, local copies, waits for them, and re-layouts, shards(): jnp.stack(jnp.split(series_mean, lax.axis_size('tm'), axis=0))  16.4 us
    another operation x3, local copies, waits for them, and re-layouts, shards(): stacked = jnp.stack([velocity_u, velocity_v], axis=1)  12.1 us
    all_to_all x1, other arithmetic, shards(): lax.all_to_all(flat_cells, 'tm', split_axis=2, concat_axis=0, tiled=True)  11.1 us
  transfers between devices with their start and end apart: 4, of which 2 were waited for; matrix products, arithmetic and copies ran while one was open for 3% of the time, Pallas kernels for 0%

profile of v1, /device:TPU:0, one launch (start us, length us, event | category | flops | bytes accessed | tf_op | source)
XLA Modules:
  0.0 284.1 jit_solution(18333886270696611892)
XLA Ops:
  0.6 2.7 stack.45
  6.9 8.0 %copy.54 = f32[48,2,8192]{0,1,2:T(2,128)} copy(f32[48,2,8192]{2,0,1:T(8,128)S(1)} %pad_maximum_fusion) | data formatting | bytes 6291456 | tf_op jit(solution)/shard_map/stack | solution.py:67
  14.8 16.1 %reshape.65 = f32[8,1,98304]{2,1,0:T(1,128)} reshape(f32[8192,2,48]{2,1,0:T(2,128)} %bitcast.47) | data formatting | bytes 6291456
  31.0 5.7 %all-to-all-start = ((f32[8,1,98304]{2,1,0:T(1,128)}), f32[8,1,98304]{2,1,0:T(1,128)S(1)}, u32[]{:S(2)}, u32[]{:S(2)}) async-start(f32[8,1,98304]{2,1,0:T(1,128)} %reshape.65), calls=%async_computation | async-start | bytes 6291456 | tf_op jit(solution)/shard_map/all_to_all | solution.py:71
  37.4 36.6 %all-to-all-done = f32[8,1,98304]{2,1,0:T(1,128)S(1)} async-done(((f32[8,1,98304]{2,1,0:T(1,128)}), f32[8,1,98304]{2,1,0:T(1,128)S(1)}, u32[]{:S(2)}, u32[]{:S(2)}) %all-to-all-start) | async-done | bytes 3145760 | tf_op jit(solution)/shard_map/all_to_all | solution.py:71
  74.5 11.1 %reduce = f32[8,98304]{1,0:T(8,128)} reduce(f32[8,1,98304]{2,1,0:T(1,128)S(1)} %all-to-all-done, f32[]{:T(128)} %broadcast.65), dimensions={1}, to_apply=%all_to_all.14.reduce_sub_computation | reduce | bytes 6291460 | tf_op jit(solution)/shard_map/all_to_all | solution.py:71
  85.6 19.0 %reshape.66 = f32[8192,2,48]{2,1,0:T(2,128)} reshape(f32[8,98304]{1,0:T(8,128)} %reduce) | data formatting | bytes 6291456
  104.6 7.0 %copy.63 = f32[48,2,8,1024]{3,2,0,1:T(8,128)S(1)} copy(f32[48,2,8,1024]{0,1,3,2:T(2,128)} %bitcast.48) | data formatting | bytes 6291456 | tf_op jit(solution)/shard_map/all_to_all | solution.py:71
  111.6 2.4 copy.56
  115.9 33.7 %while.11 = (s32[]{:T(128)}, f32[8,48,2048]{2,1,0:T(8,128)}, s32[8]{0:T(128)S(1)}, f32[432,2048]{1,0:T(8,128)S(1)}, f32[48,96]{1,0:T(8,128)}, /*index=5*/f32[432...) while((s32[]{:T(128)}, f32[8,48,2048]{2,1,0:T(8,128)}, s32[8]{0:T(128)S(1)}, ...), condition=%wide.region_1.3_spmd.clone, body=%wide.region_0.2_spmd.clone.sunk | while | flops 113399816 | bytes 1224551 | solution.py:47
  149.5 3.2 %fusion.48 = (f32[1,48,2048]{2,1,0:T(8,128)}, f32[1,48,2048]{2,1,0:T(8,128)}, f32[1,48,2048]{2,1,0:T(8,128)S(1)}, f32[1,48,2048]{2,1,0:T(8,128)}, f32[1,48,2048]...) fusion(f32[8,48,2048]{2,1,0:T(8,128)} %get-tuple-element.38), kind=kLoop, calls=%fused_computation.94 | loop fusion | bytes 6291456 | tf_op jit(solution)/shard_map/split | solution.py:74
  172.1 2.6 copy.57
  174.7 3.8 %all-to-all-start.1 = ((f32[8,48,2,1024]{3,1,2,0:T(8,128)}), f32[8,48,2,1024]{3,1,2,0:T(8,128)S(1)}, u32[]{:S(2)}, u32[]{:S(2)}) async-start(f32[8,48,2,1024]{3,1,2,0:T(8,128)} %copy.57), calls=%async_computation.1 | async-start | bytes 6291456 | tf_op jit(solution)/shard_map/all_to_all | solution.py:74
  178.6 37.7 %all-to-all-done.1 = f32[8,48,2,1024]{3,1,2,0:T(8,128)S(1)} async-done(((f32[8,48,2,1024]{3,1,2,0:T(8,128)}), f32[8,48,2,1024]{3,1,2,0:T(8,128)S(1)}, u32[]{:S(2)}, u32[]{:S(2)}) %all-to-all-start.1) | async-done | bytes 3145760 | tf_op jit(solution)/shard_map/all_to_all | solution.py:74
  216.3 3.5 %copy.58 = f32[48,2,8,1024]{3,2,1,0:T(8,128)} copy(f32[48,2,8,1024]{3,0,1,2:T(8,128)S(1)} %bitcast.49) | data formatting | bytes 6291456 | tf_op jit(solution)/shard_map/reshape | solution.py:73
  219.8 4.8 %reshape_reshape.4 = f32[48,2,2,16,256]{4,3,2,1,0:T(8,128)} reshape(f32[48,2,8,1024]{3,2,1,0:T(8,128)} %copy.58) | data formatting | bytes 6291456 | tf_op jit(solution)/shard_map/reshape;reshape | solution.py:77
  224.6 5.7 %maximum_subtract_fusion = (f32[48,2,2,16,256]{4,3,2,1,0:T(8,128)}, f32[48,2,2,16,256]{4,3,2,1,0:T(8,128)S(1)}) fusion(f32[48,2,2,16,256]{4,3,2,1,0:T(8,128)} %reshape_reshape.4, f32[48,1,2,16,256]{4,3,2,1,0:T(8,128)} %bitcast.53, f32[48,1,2,16,256]{4,3,2,1,0:T(8,128)} %bitcast.54, f32[2,16,256]{2,1,0:T(8,128)S(1)} %fusion.15), kind=kLoop, calls=%fused_computation.12 | loop fusion | flops 2359296 | bytes 12615680 | tf_op jit(solution)/shard_map/sub | solution.py:78
  230.3 3.7 %fusion.47 = (f32[48,2,2,16,255]{4,3,2,1,0:T(8,128)}, f32[48,2,2,16,255]{4,3,2,1,0:T(8,128)}) fusion(f32[48,2,2,16,256]{4,3,2,1,0:T(8,128)S(1)} %get-tuple-element.72), kind=kLoop, calls=%fused_computation.93 | loop fusion | bytes 12533760 | tf_op jit(solution)/shard_map/slice | solution.py:86
  242.0 4.8 %collective-permute-start.1 = (f32[48,2,2,16,1]{0,3,4,2,1:T(8,128)S(1)}, f32[48,2,2,16,1]{0,3,4,2,1:T(8,128)S(1)}, u32[]{:S(2)}, u32[]{:S(2)}) collective-permute-start(f32[48,2,2,16,1]{0,3,4,2,1:T(8,128)S(1)} %copy.61), channel_id=1, source_target_pairs={{0,1},{1,2},{2,3},{4,5},{5,6},{6,7},{8,9},{9,10},{10,11},{12,13},{... | collective-permute-start | bytes 36872 | tf_op jit(solution)/shard_map/ppermute | solution.py:18
  246.8 2.4 fusion.7
  249.2 2.4 copy.60
  251.6 2.4 copy.62
  254.0 4.3 %fusion.8 = f32[48,2,2,16,256]{4,3,2,1,0:T(8,128)S(1)} fusion(f32[48,2,2,16,1]{4,3,2,1,0:T(8,128)} %copy.60, f32[48,2,2,16,255]{4,3,2,1,0:T(8,128)} %get-tuple-element.76, f32[48,2,2,16,255]{4,3,2,1,0:T(8,128)S(1)} %copy-done.2, f32[48,2,2,16,1]{4,3,2,1,0:T(8,128)} %copy.62, f32[16,256]{1,0:T(8,128)S(1)} %broadcast_divide_fusion.1), kind=kLoop, calls=%fused_computation.15 | loop fusion | flops 3145728 | bytes 9453568 | tf_op jit(solution)/shard_map/mul | solution.py:87
  260.8 22.3 %psum.7 = f32[2,16,256]{2,1,0:T(8,128)S(1)} all-reduce(f32[2,16,256]{2,1,0:T(8,128)S(1)} %get-tuple-element.69), channel_id=1, replica_groups=mesh['tm'=8,'tile'=4] {'tm'}, use_global_device_ids=true, to_apply=%region_3.5 | all-reduce | flops 8192 | bytes 65536 | tf_op jit(solution)/shard_map/psum | solution.py:98
  (83 shorter events, 66.0 us)
Async XLA Ops:
  0.6 2.7 copy-start.3
  31.0 43.1 %all-to-all-start = ((f32[8,1,98304]{2,1,0:T(1,128)}), f32[8,1,98304]{2,1,0:T(1,128)S(1)}, u32[]{:S(2)}, u32[]{:S(2)}) async-start(f32[8,1,98304]{2,1,0:T(1,128)} %reshape.65), calls=%async_computation | async-start | bytes 6291456 | tf_op jit(solution)/shard_map/all_to_all | solution.py:71
  167.6 4.3 %copy-start.5 = (f32[1,48,2,1024]{3,2,1,0:T(2,128)S(1)}, f32[1,48,2,1024]{3,2,1,0:T(2,128)}, u32[]{:S(2)}) copy-start(f32[1,48,2,1024]{3,2,1,0:T(2,128)} %stack.53) | copy-start | bytes 1179652
  167.6 4.4 %copy-start.4 = (f32[1,48,2,1024]{3,2,1,0:T(2,128)S(1)}, f32[1,48,2,1024]{3,2,1,0:T(2,128)}, u32[]{:S(2)}) copy-start(f32[1,48,2,1024]{3,2,1,0:T(2,128)} %stack.55) | copy-start | bytes 1179652
  174.7 3.8 %copy-start.7 = (s32[16,256]{1,0:T(8,128)S(1)}, s32[16,256]{1,0:T(8,128)}, u32[]{:S(2)}) copy-start(s32[16,256]{1,0:T(8,128)} %param.11) | copy-start | bytes 49156
  174.7 3.8 %copy-start.8 = (f32[16,256]{1,0:T(8,128)S(1)}, f32[16,256]{1,0:T(8,128)}, u32[]{:S(2)}) copy-start(f32[16,256]{1,0:T(8,128)} %param.13) | copy-start | bytes 49156
  174.7 3.9 %copy-start.9 = (f32[16,256]{1,0:T(8,128)S(1)}, f32[16,256]{1,0:T(8,128)}, u32[]{:S(2)}) copy-start(f32[16,256]{1,0:T(8,128)} %param.14) | copy-start | bytes 49156
  174.7 3.9 %copy-start.6 = (s32[16,256]{1,0:T(8,128)S(1)}, s32[16,256]{1,0:T(8,128)}, u32[]{:S(2)}) copy-start(s32[16,256]{1,0:T(8,128)} %param.12) | copy-start | bytes 49156
  174.7 41.6 %all-to-all-start.1 = ((f32[8,48,2,1024]{3,1,2,0:T(8,128)}), f32[8,48,2,1024]{3,1,2,0:T(8,128)S(1)}, u32[]{:S(2)}, u32[]{:S(2)}) async-start(f32[8,48,2,1024]{3,1,2,0:T(8,128)} %copy.57), calls=%async_computation.1 | async-start | bytes 6291456 | tf_op jit(solution)/shard_map/all_to_all | solution.py:74
  238.5 10.7 %collective-permute-start = (f32[48,2,2,16,1]{0,3,4,2,1:T(8,128)S(1)}, f32[48,2,2,16,1]{0,3,4,2,1:T(8,128)S(1)}, u32[]{:S(2)}, u32[]{:S(2)}) collective-permute-start(f32[48,2,2,16,1]{0,3,4,2,1:T(8,128)S(1)} %copy.59), channel_id=1, source_target_pairs={{1,0},{2,1},{3,2},{5,4},{6,5},{7,6},{9,8},{10,9},{11,10},{13,12},{... | collective-permute-start | bytes 36872 | tf_op jit(solution)/shard_map/ppermute | solution.py:19
  242.0 9.6 %collective-permute-start.1 = (f32[48,2,2,16,1]{0,3,4,2,1:T(8,128)S(1)}, f32[48,2,2,16,1]{0,3,4,2,1:T(8,128)S(1)}, u32[]{:S(2)}, u32[]{:S(2)}) collective-permute-start(f32[48,2,2,16,1]{0,3,4,2,1:T(8,128)S(1)} %copy.61), channel_id=1, source_target_pairs={{0,1},{1,2},{2,3},{4,5},{5,6},{6,7},{8,9},{9,10},{10,11},{12,13},{... | collective-permute-start | bytes 36872 | tf_op jit(solution)/shard_map/ppermute | solution.py:18
  249.2 4.7 %copy-start.2 = (f32[48,2,2,16,255]{4,3,2,1,0:T(8,128)S(1)}, f32[48,2,2,16,255]{4,3,2,1,0:T(8,128)}, u32[]{:S(2)}) copy-start(f32[48,2,2,16,255]{4,3,2,1,0:T(8,128)} %get-tuple-element.75) | copy-start | bytes 9400324
  254.0 4.3 %copy-start = (f32[48,2,2,16,256]{4,3,2,1,0:T(8,128)S(1)}, f32[48,2,2,16,256]{4,3,2,1,0:T(8,128)}, u32[]{:S(2)}) copy-start(f32[48,2,2,16,256]{4,3,2,1,0:T(8,128)} %fusion.7) | copy-start | bytes 9437188
  254.0 4.7 %copy-start.1 = (f32[48,2,2,16,256]{4,3,2,1,0:T(8,128)S(1)}, f32[48,2,2,16,256]{4,3,2,1,0:T(8,128)}, u32[]{:S(2)}) copy-start(f32[48,2,2,16,256]{4,3,2,1,0:T(8,128)} %get-tuple-element.71) | copy-start | bytes 9437188
